TPU v7x, 32 devices: a whole 2x2x4 slice. The times are simulated.
32 devices in a mesh: dp: 8 (over z, y), tensor: 4 (over x, core).
Axes of the slice: x: 2, y: 2, z: 4, core: 2. Of those that a mesh axis runs over, the one named last changes fastest.
Arguments:
- tokens: bfloat16 [8192, 768], P(('dp', 'tensor')), may hold values from -6 to 6
- gain_attn: bfloat16 [768], P('dp'), may hold values from 0.5 to 1.5
- gain_mlp: bfloat16 [768], P('dp'), may hold values from 0.5 to 1.5
- w_qkv: bfloat16 [3, 768, 768], P(None, 'dp', 'tensor'), may hold values from -0.3125 to 0.3125
- w_out: bfloat16 [768, 768], P('tensor', 'dp'), may hold values from -0.875 to 0.875
- w_in: bfloat16 [2, 768, 1152], P(None, 'dp', 'tensor'), may hold values from -0.21875 to 0.21875
- w_down: bfloat16 [1152, 768], P('tensor', 'dp'), may hold values from -0.1875 to 0.1875
- cotangent: bfloat16 [8192, 768], P(('dp', 'tensor')), may hold values from -6 to 6
Outputs:
- mixed: bfloat16 [8192, 768], P(('dp', 'tensor'))
- input_grad: float32 [8192, 768], P(('dp', 'tensor'))
- grad_gain_attn: float32 [768], P('dp')
- grad_gain_mlp: float32 [768], P('dp')
- grad_qkv: float32 [3, 768, 768], P(None, 'dp', 'tensor')
- grad_out: float32 [768, 768], P('tensor', 'dp')
- grad_in: float32 [2, 768, 1152], P(None, 'dp', 'tensor')
- grad_down: float32 [1152, 768], P('tensor', 'dp')
All inputs are finite; a program needn't handle non-finite values.
Results may differ from a plain program's by a relative error of at most 0.018.
The roundings to bfloat16 on the way count: a program that leaves them out, or rounds other values in their place, can miss the bound.
Values may be sent and summed in bfloat16 or wider, within the bound.
A program may use at most 128 MiB of HBM per device.

v0:
```python
import jax
import jax.numpy as jnp
from jax import lax
from jax.sharding import PartitionSpec as P

HEAD = 64
LEN = 1024


epsilon = 1e-05
rope_base = 160000.0


def cut_along(array, dim, length):
    dims = array.shape
    pieces = array.reshape(*dims[:dim], length, dims[dim] // length, *dims[dim + 1 :])
    return jnp.moveaxis(pieces, dim, 0)


def summed_on_arrival(array, axis, dim):
    pieces = cut_along(array, dim, lax.axis_size(axis))
    arrived = lax.all_to_all(pieces, axis, split_axis=0, concat_axis=0, tiled=True)
    return arrived.astype(jnp.float32).sum(axis=0)


def gelu_exact(inputs):
    return 0.5 * inputs * (1.0 + jax.scipy.special.erf(inputs * 0.7071067811865476))


def glu_mix(gate_up):
    return gelu_exact(gate_up[0]) * gate_up[1]


def norm_rows(inputs, gain):
    centred = inputs - jnp.mean(inputs, axis=-1, keepdims=True)
    spread = jnp.mean(centred * centred, axis=-1, keepdims=True)
    return centred * lax.rsqrt(spread + epsilon) * gain


def rotary(length):
    half_size = HEAD // 2
    frequency = rope_base ** (-2.0 * jnp.arange(half_size, dtype=jnp.float32) / HEAD)
    angles = jnp.arange(length, dtype=jnp.float32)[:, None] * frequency[None, :]
    return (jnp.cos(angles)[:, None, :], jnp.sin(angles)[:, None, :])


def rotate(inputs, cosine, sine_table):
    half_size = inputs.shape[-1] // 2
    first_half = inputs[..., :half_size]
    second = inputs[..., half_size:]
    return jnp.concatenate(
        [first_half * cosine - second * sine_table, second * cosine + first_half * sine_table],
        axis=-1,
    )


def rotate_back(inputs, cosine, sine_table):
    half_size = inputs.shape[-1] // 2
    first_half = inputs[..., :half_size]
    second = inputs[..., half_size:]
    return jnp.concatenate(
        [first_half * cosine + second * sine_table, second * cosine - first_half * sine_table],
        axis=-1,
    )


def per_device(tokens, gain_attn, gain_mlp, w_qkv, w_out, w_in, w_down, cotangent):
    row_count = tokens.shape[0]
    group_rows = row_count * lax.axis_size("tensor")
    seq_count = group_rows // LEN
    block_rows = min(512, LEN)
    block_count = LEN // block_rows
    score_scale = HEAD ** (-0.5)
    inputs = tokens.astype(jnp.float32)
    gain_one, gain_two, qkv_weight, out_weight, in_weight, down_weight = (
        lax.all_gather(gain_attn, "dp", axis=0, tiled=True),
        lax.all_gather(gain_mlp, "dp", axis=0, tiled=True),
        lax.all_gather(w_qkv, "dp", axis=1, tiled=True),
        lax.all_gather(w_out, "dp", axis=1, tiled=True),
        lax.all_gather(w_in, "dp", axis=1, tiled=True),
        lax.all_gather(w_down, "dp", axis=1, tiled=True),
    )
    local_width = qkv_weight.shape[2]
    local_heads = local_width // HEAD
    cosine, sine_table = rotary(LEN)

    def split_blocks(array):
        return array.reshape(seq_count, block_count, block_rows, local_heads, HEAD).transpose(
            1, 0, 2, 3, 4
        )

    def join_blocks(array):
        return array.transpose(1, 0, 2, 3, 4).reshape(seq_count, LEN, local_heads, HEAD)

    normed_attn = norm_rows(inputs, gain_one.astype(jnp.float32)).astype(jnp.bfloat16)
    attn_rows = lax.all_gather(normed_attn, "tensor", axis=0, tiled=True)
    projected = jnp.einsum("td,cde->cte", attn_rows, qkv_weight, preferred_element_type=jnp.float32)
    shaped = projected.reshape(3, seq_count, LEN, local_heads, HEAD)
    queries = rotate(shaped[0], cosine, sine_table).astype(jnp.bfloat16)
    keys_rot = rotate(shaped[1], cosine, sine_table).astype(jnp.bfloat16)
    values = shaped[2].astype(jnp.bfloat16)

    def attend(query_block):
        scores = (
            jnp.einsum("sqhd,skhd->shqk", query_block, keys_rot, preferred_element_type=jnp.float32)
            * score_scale
        )
        row_max = jnp.max(scores, axis=-1, keepdims=True)
        weights = jnp.exp(scores - row_max)
        row_total = jnp.sum(weights, axis=-1, keepdims=True)
        prob_block = (weights / row_total).astype(jnp.bfloat16)
        result = jnp.einsum(
            "shqk,skhd->sqhd", prob_block, values, preferred_element_type=jnp.float32
        )
        return (result.astype(jnp.bfloat16), (row_max + jnp.log(row_total))[..., 0])

    query_blocks = split_blocks(queries)
    attn_blocks, log_totals = lax.map(attend, query_blocks)
    attended = join_blocks(attn_blocks).reshape(group_rows, local_width)
    mixed_attn = inputs + lax.psum_scatter(
        jnp.dot(attended, out_weight, preferred_element_type=jnp.float32),
        "tensor",
        scatter_dimension=0,
        tiled=True,
    )
    normed_mlp = norm_rows(mixed_attn, gain_two.astype(jnp.float32)).astype(jnp.bfloat16)
    mlp_rows = lax.all_gather(normed_mlp, "tensor", axis=0, tiled=True)
    gate_up = jnp.einsum("td,cdf->ctf", mlp_rows, in_weight, preferred_element_type=jnp.float32)
    hidden = glu_mix(gate_up).astype(jnp.bfloat16)
    output = mixed_attn + lax.psum_scatter(
        jnp.dot(hidden, down_weight, preferred_element_type=jnp.float32).astype(jnp.bfloat16),
        "tensor",
        scatter_dimension=0,
        tiled=True,
    ).astype(jnp.float32)
    mixed_out = output.astype(jnp.bfloat16)
    grad_out_rows = lax.all_gather(cotangent, "tensor", axis=0, tiled=True)
    grad_down = jnp.einsum("tf,td->fd", hidden, grad_out_rows, preferred_element_type=jnp.float32)
    grad_hidden = jnp.einsum(
        "td,fd->tf", grad_out_rows, down_weight, preferred_element_type=jnp.float32
    )
    unused_glu, glu_pull = jax.vjp(glu_mix, gate_up)
    grad_gate_up = glu_pull(grad_hidden)[0].astype(jnp.bfloat16)
    grad_in = jnp.einsum("td,ctf->cdf", mlp_rows, grad_gate_up, preferred_element_type=jnp.float32)
    grad_normed_mlp = lax.psum_scatter(
        jnp.einsum(
            "ctf,cdf->td", grad_gate_up, in_weight, preferred_element_type=jnp.float32
        ).astype(jnp.bfloat16),
        "tensor",
        scatter_dimension=0,
        tiled=True,
    ).astype(jnp.float32)
    unused_mlp, norm_pull_mlp = jax.vjp(norm_rows, mixed_attn, gain_two.astype(jnp.float32))
    grad_mixed_part, grad_gain_two = norm_pull_mlp(grad_normed_mlp)
    grad_mixed = cotangent.astype(jnp.float32) + grad_mixed_part
    grad_branch = grad_mixed.astype(jnp.bfloat16)
    branch_rows = lax.all_gather(grad_branch, "tensor", axis=0, tiled=True)
    grad_out_weight = jnp.einsum(
        "te,td->ed", attended, branch_rows, preferred_element_type=jnp.float32
    )
    grad_attended = jnp.einsum(
        "td,ed->te", branch_rows, out_weight, preferred_element_type=jnp.float32
    ).astype(jnp.bfloat16)

    def attend_back(state_pair, block_items):
        grad_keys, grad_values = state_pair
        query_block, grad_block, log_block = block_items
        scores = (
            jnp.einsum("sqhd,skhd->shqk", query_block, keys_rot, preferred_element_type=jnp.float32)
            * score_scale
        )
        prob_block = jnp.exp(scores - log_block[..., None])
        grad_probs = jnp.einsum(
            "sqhd,skhd->shqk", grad_block, values, preferred_element_type=jnp.float32
        )
        inner_sum = jnp.sum(prob_block * grad_probs, axis=-1, keepdims=True)
        grad_scores = (prob_block * (grad_probs - inner_sum)).astype(jnp.bfloat16)
        grad_query = (
            jnp.einsum("shqk,skhd->sqhd", grad_scores, keys_rot, preferred_element_type=jnp.float32)
            * score_scale
        )
        grad_keys = (
            grad_keys
            + jnp.einsum(
                "shqk,sqhd->skhd", grad_scores, query_block, preferred_element_type=jnp.float32
            )
            * score_scale
        )
        grad_values = grad_values + jnp.einsum(
            "shqk,sqhd->skhd",
            prob_block.astype(jnp.bfloat16),
            grad_block,
            preferred_element_type=jnp.float32,
        )
        return ((grad_keys, grad_values), grad_query)

    zero_state = jnp.zeros((seq_count, LEN, local_heads, HEAD), jnp.float32)
    (grad_keys, grad_values), grad_queries = lax.scan(
        attend_back,
        (zero_state, zero_state),
        (query_blocks, split_blocks(grad_attended), log_totals),
    )
    grad_projected = (
        jnp.stack(
            [
                rotate_back(join_blocks(grad_queries), cosine, sine_table),
                rotate_back(grad_keys, cosine, sine_table),
                grad_values,
            ]
        )
        .reshape(3, group_rows, local_width)
        .astype(jnp.bfloat16)
    )
    grad_qkv = jnp.einsum(
        "td,cte->cde", attn_rows, grad_projected, preferred_element_type=jnp.float32
    )
    grad_normed_attn = lax.psum_scatter(
        jnp.einsum(
            "cte,cde->td", grad_projected, qkv_weight, preferred_element_type=jnp.float32
        ).astype(jnp.bfloat16),
        "tensor",
        scatter_dimension=0,
        tiled=True,
    ).astype(jnp.float32)
    unused_attn, norm_pull_attn = jax.vjp(norm_rows, inputs, gain_one.astype(jnp.float32))
    grad_inputs_part, grad_gain_one = norm_pull_attn(grad_normed_attn)
    input_grad = grad_mixed + grad_inputs_part
    gain_sums = lax.psum(jnp.stack([grad_gain_one, grad_gain_two]), "tensor")
    gain_part, qkv_part, out_part, in_part, down_part = (
        summed_on_arrival(gain_sums.astype(jnp.bfloat16), "dp", 1),
        summed_on_arrival(grad_qkv.astype(jnp.bfloat16), "dp", 1),
        summed_on_arrival(grad_out_weight.astype(jnp.bfloat16), "dp", 1),
        summed_on_arrival(grad_in.astype(jnp.bfloat16), "dp", 1),
        summed_on_arrival(grad_down.astype(jnp.bfloat16), "dp", 1),
    )
    return (
        mixed_out,
        input_grad,
        gain_part[0],
        gain_part[1],
        qkv_part,
        out_part,
        in_part,
        down_part,
    )


def solution(mesh):
    placed = (
        P(("dp", "tensor"), None),
        P("dp"),
        P("dp"),
        P(None, "dp", "tensor"),
        P("tensor", "dp"),
        P(None, "dp", "tensor"),
        P("tensor", "dp"),
        P(("dp", "tensor"), None),
    )
    return jax.shard_map(
        per_device,
        mesh=mesh,
        in_specs=placed,
        out_specs=(
            P(("dp", "tensor"), None),
            P(("dp", "tensor"), None),
            P("dp"),
            P("dp"),
            P(None, "dp", "tensor"),
            P("tensor", "dp"),
            P(None, "dp", "tensor"),
            P("tensor", "dp"),
        ),
        check_vma=False,
    )
```

profile of v0, /device:TPU:0, one launch (start us, length us, event | category | flops | bytes accessed | tf_op | source)
XLA Modules:
  0.0 484.4 jit_solution(4716086893156739680)
XLA Ops:
  13.3 23.1 %all-reduce.4 = (bf16[768]{0:T(1024)(128)(2,1)S(1)}, bf16[768]{0:T(1024)(128)(2,1)S(1)}) all-reduce(bf16[768]{0:T(1024)(128)(2,1)S(1)} %dynamic-update-slice, bf16[768]{0:T(1024)(128)(2,1)S(1)} %dynamic-update-slice.1), channel_id=1, replica_groups=mesh['dp'=8,'tensor'=4] {'dp'}, use_global_device_ids=true, to_apply=%add.2 | all-reduce | flops 1536 | bytes 6144
  38.8 35.2 %all_gather.32 = bf16[3,768,192]{2,0,1:T(4,128)(2,1)S(1)} all-gather(bf16[3,96,192]{2,0,1:T(4,128)(2,1)S(1)} %copy.53), channel_id=1, replica_groups=mesh['dp'=8,'tensor'=4] {'dp'}, dimensions={1}, use_global_device_ids=true | all-gather | bytes 995328 | tf_op jit(solution)/shard_map/all_gather | solution.py:78
  74.9 31.0 %all_gather.33 = bf16[192,768]{0,1:T(8,128)(2,1)S(1)} all-gather(bf16[192,96]{0,1:T(8,128)(2,1)S(1)} %copy.58), channel_id=1, replica_groups=mesh['dp'=8,'tensor'=4] {'dp'}, dimensions={1}, use_global_device_ids=true | all-gather | bytes 331776 | tf_op jit(solution)/shard_map/all_gather | solution.py:79
  109.7 8.6 %while.27 = (s32[]{:T(128)}, bf16[2,1,512,3,64]{2,4,3,1,0:T(8,128)(2,1)S(1)}, f32[2,1,3,512]{3,2,1,0:T(4,128)S(1)}, bf16[2,1,512,3,64]{2,4,3,1,0:T(8,128)(2,1)S(...) while((s32[]{:T(128)}, ...), condition=%wide.region_5.6_spmd, body=%wide.region_2.5_spmd.sunk | while | flops 416905728 | bytes 20113504 | solution.py:118
  121.9 37.8 %reduce-scatter.5.cloned.1.call-done = f32[256,768]{1,0:T(8,128)} async-done(((f32[1024,768]{1,0:T(8,128)}), f32[256,768]{1,0:T(8,128)}) %reduce-scatter.5.cloned.1.call-update) | async-done | bytes 786448 | tf_op jit(solution)/shard_map/reduce_scatter | solution.py:120
  163.2 33.8 %all_gather.37 = bf16[288,768]{0,1:T(8,128)(2,1)} all-gather(bf16[288,96]{0,1:T(8,128)(2,1)S(1)} %copy.61), channel_id=1, replica_groups=mesh['dp'=8,'tensor'=4] {'dp'}, dimensions={1}, use_global_device_ids=true | all-gather | bytes 497664 | tf_op jit(solution)/shard_map/all_gather | solution.py:81
  196.9 34.9 %all_gather.36 = bf16[2,768,288]{2,0,1:T(2,128)(2,1)S(1)} all-gather(bf16[2,96,288]{2,0,1:T(2,128)(2,1)S(1)} %copy.59), channel_id=1, replica_groups=mesh['dp'=8,'tensor'=4] {'dp'}, dimensions={1}, use_global_device_ids=true | all-gather | bytes 995328 | tf_op jit(solution)/shard_map/all_gather | solution.py:80
  231.8 4.0 convolution_bitcast_fusion
  235.8 4.3 multiply_bitcast_fusion
  245.4 3.3 convolution_convert_fusion
  248.7 23.5 %reduce-scatter.9.cloned.1.call-done = bf16[256,768]{1,0:T(8,128)(2,1)} async-done(((bf16[1024,768]{1,0:T(8,128)(2,1)}), bf16[256,768]{1,0:T(8,128)(2,1)}) %reduce-scatter.9.cloned.1.call-update) | async-done | bytes 393232 | tf_op jit(solution)/shard_map/reduce_scatter | solution.py:145
  274.8 28.0 %reduce-scatter.7.cloned.1.call-done = bf16[256,768]{1,0:T(8,128)(2,1)} async-done(((bf16[1024,768]{1,0:T(8,128)(2,1)}), bf16[256,768]{1,0:T(8,128)(2,1)}) %reduce-scatter.7.cloned.1.call-update) | async-done | bytes 393232 | tf_op jit(solution)/shard_map/reduce_scatter | solution.py:130
  306.6 3.0 convolution_convert_fusion.1
  314.1 5.5 %all-to-all-start.4 = ((bf16[8,288,96]{2,1,0:T(8,128)(2,1)}), bf16[8,288,96]{2,1,0:T(8,128)(2,1)}, u32[]{:S(2)}, u32[]{:S(2)}) async-start(bf16[8,288,96]{2,1,0:T(8,128)(2,1)} %bitcast.242), calls=%async_computation.8 | async-start | bytes 1179648 | tf_op jit(solution)/shard_map/all_to_all | solution.py:22
  319.6 4.1 fusion.58
  323.7 3.2 reshape.359
  329.5 2.8 convolution_convert_fusion.2
  334.4 36.4 %while.28 = (s32[]{:T(128)}, f32[1,1024,3,64]{1,3,2,0:T(8,128)S(1)}, f32[1,1024,3,64]{1,3,2,0:T(8,128)S(1)}, f32[2,1,512,3,64]{2,0,4,3,1:T(2,128)}, bf16[2,1,512...) while((s32[]{:T(128)}, ...), condition=%wide.region_15.16_spmd.clone, body=%wide.region_13.15_spmd.clone.sunk | while | flops 1026587136 | bytes 54306964 | solution.py:198
  337.8 2.9 multiply_reduce_fusion.6
  344.5 8.1 %dynamic_update_slice.20 = f32[2,1,512,3,64]{2,0,4,3,1:T(2,128)} dynamic-update-slice(f32[2,1,512,3,64]{2,0,4,3,1:T(2,128)} %get-tuple-element.380, f32[1,1,512,3,64]{2,0,4,3,1:T(1,128)S(1)} %copy.114, s32[]{:T(128)S(6)} %copy.134, s32[]{:T(128)} %constant.36.clone.1..sunk, s32[]{:T(128)} %constant.36.clone.1..sunk, s32[]{:T(128)} %constant.36.clone.1..sunk, s32[]{:T(128)} %constant.36.clone.1..sunk) | dynamic-update-slice | bytes 786436 | tf_op jit(solution)/shard_map/while/body/jit(dynamic_update_index_in_dim)/dynamic_update_slice | solution.py:198
  356.0 2.9 multiply_reduce_fusion.6
  362.7 8.1 %dynamic_update_slice.20 = f32[2,1,512,3,64]{2,0,4,3,1:T(2,128)} dynamic-update-slice(f32[2,1,512,3,64]{2,0,4,3,1:T(2,128)} %get-tuple-element.380, f32[1,1,512,3,64]{2,0,4,3,1:T(1,128)S(1)} %copy.114, s32[]{:T(128)S(6)} %copy.134, s32[]{:T(128)} %constant.36.clone.1..sunk, s32[]{:T(128)} %constant.36.clone.1..sunk, s32[]{:T(128)} %constant.36.clone.1..sunk, s32[]{:T(128)} %constant.36.clone.1..sunk) | dynamic-update-slice | bytes 786436 | tf_op jit(solution)/shard_map/while/body/jit(dynamic_update_index_in_dim)/dynamic_update_slice | solution.py:198
  374.3 6.1 %all-to-all-start.3 = ((bf16[8,2,96,288]{2,3,1,0:T(8,128)(2,1)}), bf16[8,2,96,288]{2,3,1,0:T(8,128)(2,1)S(1)}, u32[]{:S(2)}, u32[]{:S(2)}) async-start(bf16[8,2,96,288]{2,3,1,0:T(8,128)(2,1)} %bitcast.197), calls=%async_computation.7 | async-start | bytes 2359296 | tf_op jit(solution)/shard_map/all_to_all | solution.py:22
  389.6 19.0 %all-to-all-done.3 = bf16[8,2,96,288]{2,3,1,0:T(8,128)(2,1)S(1)} async-done(((bf16[8,2,96,288]{2,3,1,0:T(8,128)(2,1)}), bf16[8,2,96,288]{2,3,1,0:T(8,128)(2,1)S(1)}, u32[]{:S(2)}, u32[]{:S(2)}) %all-to-all-start.3) | async-done | bytes 884768 | tf_op jit(solution)/shard_map/all_to_all | solution.py:22
  408.6 3.5 all-to-all-start.2
  412.1 3.4 fusion.55
  419.2 4.6 all-to-all-done.2
  423.8 3.6 all-to-all-start.1
  431.2 24.9 %all-to-all-done.1 = bf16[8,3,96,192]{2,3,1,0:T(8,128)(2,1)S(1)} async-done(((bf16[8,3,96,192]{2,3,1,0:T(8,128)(2,1)}), bf16[8,3,96,192]{2,3,1,0:T(8,128)(2,1)S(1)}, u32[]{:S(2)}, u32[]{:S(2)}) %all-to-all-start.1) | async-done | bytes 884768 | tf_op jit(solution)/shard_map/all_to_all | solution.py:22
  460.2 6.1 %psum.7 = bf16[2,768]{1,0:T(2,128)(2,1)S(1)} all-reduce(f32[2,768]{1,0:T(2,128)S(1)} %pad_maximum_fusion.6), channel_id=1, replica_groups=mesh['dp'=8,'tensor'=4] {'tensor'}, use_global_device_ids=true, to_apply=%region_21.22 | all-reduce | flops 1536 | bytes 9216 | tf_op jit(solution)/shard_map/psum | solution.py:228
  467.0 3.6 all-to-all-start
  471.9 5.2 %all-to-all-done = bf16[8,2,96]{2,1,0:T(2,128)(2,1)S(1)} async-done(((bf16[8,2,96]{2,1,0:T(2,128)(2,1)}), bf16[8,2,96]{2,1,0:T(2,128)(2,1)S(1)}, u32[]{:S(2)}, u32[]{:S(2)}) %all-to-all-start) | async-done | bytes 3104 | tf_op jit(solution)/shard_map/all_to_all | solution.py:22
  (222 shorter events, 89.1 us)
Async XLA Ops:
  7.2 31.3 %copy-start.32 = (bf16[192,96]{1,0:T(8,128)(2,1)S(1)}, bf16[192,96]{1,0:T(8,128)(2,1)}, u32[]{:S(2)}) copy-start(bf16[192,96]{1,0:T(8,128)(2,1)} %param.16) | copy-start | bytes 110596
  7.2 31.5 %copy-start.26 = (bf16[3,96,192]{2,1,0:T(8,128)(2,1)S(1)}, bf16[3,96,192]{2,1,0:T(8,128)(2,1)}, u32[]{:S(2)}) copy-start(bf16[3,96,192]{2,1,0:T(8,128)(2,1)} %param.15) | copy-start | bytes 331780
  7.2 99.3 %all-gather.5.cloned.1.call-start = ((), (), s32[]{:S(2)}) async-start(), calls=%async_computation.9 | async-start | bytes 1966080 | tf_op jit(solution)/shard_map/all_gather | solution.py:96
  8.4 30.1 %copy-start.33 = (f32[256]{0:T(256)}, f32[256]{0:T(256)S(1)}, u32[]{:S(2)}) copy-start(f32[256]{0:T(256)S(1)} %broadcast_multiply_fusion.1) | copy-start | bytes 3076
  9.7 28.8 %copy-start.44 = (f32[256]{0:T(256)}, f32[256]{0:T(256)S(1)}, u32[]{:S(2)}) copy-start(f32[256]{0:T(256)S(1)} %fusion.80) | copy-start | bytes 3076
  9.7 28.8 %copy-start.37 = (f32[256]{0:T(256)}, f32[256]{0:T(256)S(1)}, u32[]{:S(2)}) copy-start(f32[256]{0:T(256)S(1)} %fusion.86) | copy-start | bytes 3076
  38.4 121.3 %reduce-scatter.5.cloned.1.call-start = ((), (), s32[]{:S(2)}) async-start(), calls=%async_computation.10 | async-start | bytes 3932160 | tf_op jit(solution)/shard_map/reduce_scatter | solution.py:120
  74.9 34.2 %copy-start.16 = (bf16[3,768,192]{1,2,0:T(8,128)(2,1)}, bf16[3,768,192]{1,2,0:T(8,128)(2,1)S(1)}, u32[]{:S(2)}) copy-start(bf16[3,768,192]{1,2,0:T(8,128)(2,1)S(1)} %copy.54) | copy-start | bytes 2654212
  121.8 37.9 %copy-start = (bf16[256,768]{1,0:T(8,128)(2,1)S(1)}, bf16[256,768]{1,0:T(8,128)(2,1)}, u32[]{:S(2)}) copy-start(bf16[256,768]{1,0:T(8,128)(2,1)} %param.12) | copy-start | bytes 1179652
  121.8 110.0 %all-gather.7.cloned.1.call-start = ((), (), s32[]{:S(2)}) async-start(), calls=%async_computation.11 | async-start | bytes 1966080 | tf_op jit(solution)/shard_map/all_gather | solution.py:127
  121.9 40.4 %copy-start.30 = (f32[768]{0:T(1024)}, f32[768]{0:T(1024)S(1)}, u32[]{:S(2)}) copy-start(f32[768]{0:T(1024)S(1)} %convert_element_type.149) | copy-start | bytes 9220
  162.3 73.6 %all-gather.9.cloned.1.call-start = ((), (), s32[]{:S(2)}) async-start(), calls=%async_computation.13 | async-start | bytes 1966080 | tf_op jit(solution)/shard_map/all_gather | solution.py:137
  162.9 109.3 %reduce-scatter.9.cloned.1.call-start = ((), (), s32[]{:S(2)}) async-start(), calls=%async_computation.14 | async-start | bytes 1966080 | tf_op jit(solution)/shard_map/reduce_scatter | solution.py:145
  244.4 58.5 %reduce-scatter.7.cloned.1.call-start = ((), (), s32[]{:S(2)}) async-start(), calls=%async_computation.12 | async-start | bytes 1966080 | tf_op jit(solution)/shard_map/reduce_scatter | solution.py:130
  245.4 26.8 %copy-start.31 = (f32[768]{0:T(1024)S(1)}, f32[768]{0:T(1024)}, u32[]{:S(2)}) copy-start(f32[768]{0:T(1024)} %copy-done.30) | copy-start | bytes 9220
  245.4 26.8 %copy-start.36 = (f32[256]{0:T(256)S(1)}, f32[256]{0:T(256)}, u32[]{:S(2)}) copy-start(f32[256]{0:T(256)} %copy-done.35) | copy-start | bytes 3076
  245.4 26.8 %copy-start.41 = (f32[256]{0:T(256)S(1)}, f32[256]{0:T(256)}, u32[]{:S(2)}) copy-start(f32[256]{0:T(256)} %copy-done.40) | copy-start | bytes 3076
  248.7 80.8 %all-gather.11.cloned.1.call-start = ((), (), s32[]{:S(2)}) async-start(), calls=%async_computation.15 | async-start | bytes 1966080 | tf_op jit(solution)/shard_map/all_gather | solution.py:157
  274.2 31.4 %copy-start.5 = (bf16[256,768]{1,0:T(8,128)(2,1)S(1)}, bf16[256,768]{1,0:T(8,128)(2,1)}, u32[]{:S(2)}) copy-start(bf16[256,768]{1,0:T(8,128)(2,1)} %param.19) | copy-start | bytes 1179652
  314.1 60.2 %all-to-all-start.4 = ((bf16[8,288,96]{2,1,0:T(8,128)(2,1)}), bf16[8,288,96]{2,1,0:T(8,128)(2,1)}, u32[]{:S(2)}, u32[]{:S(2)}) async-start(bf16[8,288,96]{2,1,0:T(8,128)(2,1)} %bitcast.242), calls=%async_computation.8 | async-start | bytes 1179648 | tf_op jit(solution)/shard_map/all_to_all | solution.py:22
  374.3 34.3 %all-to-all-start.3 = ((bf16[8,2,96,288]{2,3,1,0:T(8,128)(2,1)}), bf16[8,2,96,288]{2,3,1,0:T(8,128)(2,1)S(1)}, u32[]{:S(2)}, u32[]{:S(2)}) async-start(bf16[8,2,96,288]{2,3,1,0:T(8,128)(2,1)} %bitcast.197), calls=%async_computation.7 | async-start | bytes 2359296 | tf_op jit(solution)/shard_map/all_to_all | solution.py:22
  380.4 76.9 %reduce-scatter.11.cloned.1.call-start = ((), (), s32[]{:S(2)}) async-start(), calls=%async_computation.16 | async-start | bytes 1966080 | tf_op jit(solution)/shard_map/reduce_scatter | solution.py:217
  408.6 15.2 %all-to-all-start.2 = ((bf16[8,192,96]{2,1,0:T(8,128)(2,1)}), bf16[8,192,96]{2,1,0:T(8,128)(2,1)S(1)}, u32[]{:S(2)}, u32[]{:S(2)}) async-start(bf16[8,192,96]{2,1,0:T(8,128)(2,1)} %bitcast.200), calls=%async_computation.6 | async-start | bytes 786432 | tf_op jit(solution)/shard_map/all_to_all | solution.py:22
  423.8 32.3 %all-to-all-start.1 = ((bf16[8,3,96,192]{2,3,1,0:T(8,128)(2,1)}), bf16[8,3,96,192]{2,3,1,0:T(8,128)(2,1)S(1)}, u32[]{:S(2)}, u32[]{:S(2)}) async-start(bf16[8,3,96,192]{2,3,1,0:T(8,128)(2,1)} %bitcast.198), calls=%async_computation.5 | async-start | bytes 2359296 | tf_op jit(solution)/shard_map/all_to_all | solution.py:22
  429.6 27.7 %copy-start.28 = (f32[768]{0:T(1024)S(1)}, f32[768]{0:T(1024)}, u32[]{:S(2)}) copy-start(f32[768]{0:T(1024)} %copy-done.27) | copy-start | bytes 9220
  429.6 27.7 %copy-start.34 = (f32[256]{0:T(256)S(1)}, f32[256]{0:T(256)}, u32[]{:S(2)}) copy-start(f32[256]{0:T(256)} %copy-done.33) | copy-start | bytes 3076
  430.5 28.2 %copy-start.45 = (f32[256]{0:T(256)S(1)}, f32[256]{0:T(256)}, u32[]{:S(2)}) copy-start(f32[256]{0:T(256)} %copy-done.44) | copy-start | bytes 3076
  430.5 28.2 %copy-start.38 = (f32[256]{0:T(256)S(1)}, f32[256]{0:T(256)}, u32[]{:S(2)}) copy-start(f32[256]{0:T(256)} %copy-done.37) | copy-start | bytes 3076
  431.2 39.4 %copy-start.2 = (f32[256,768]{1,0:T(8,128)S(1)}, f32[256,768]{1,0:T(8,128)}, u32[]{:S(2)}) copy-start(f32[256,768]{1,0:T(8,128)} %copy-done.1) | copy-start | bytes 2359300
  431.2 39.4 %copy-start.6 = (bf16[256,768]{1,0:T(8,128)(2,1)S(1)}, bf16[256,768]{1,0:T(8,128)(2,1)}, u32[]{:S(2)}) copy-start(bf16[256,768]{1,0:T(8,128)(2,1)} %param.19) | copy-start | bytes 1179652
  431.2 39.4 %copy-start.43 = (f32[256]{0:T(256)S(1)}, f32[256]{0:T(256)}, u32[]{:S(2)}) copy-start(f32[256]{0:T(256)} %copy-done.42) | copy-start | bytes 3076
  467.0 10.0 %all-to-all-start = ((bf16[8,2,96]{2,1,0:T(2,128)(2,1)}), bf16[8,2,96]{2,1,0:T(2,128)(2,1)S(1)}, u32[]{:S(2)}, u32[]{:S(2)}) async-start(bf16[8,2,96]{2,1,0:T(2,128)(2,1)} %copy.66), calls=%async_computation.4 | async-start | bytes 8192 | tf_op jit(solution)/shard_map/all_to_all | solution.py:22
  (31 other events, 184.0 us)
Sparse Core Ops, SparseCore 0:
  38.5 16.9 all-gather.4
  121.9 37.7 reduce-scatter.4
  162.4 19.6 all-gather.6
  183.6 19.6 all-gather.8
  244.5 27.6 reduce-scatter.8
  274.6 28.1 reduce-scatter.6
  306.7 19.6 all-gather.10
  384.8 28.3 reduce-scatter.10
where the time goes:
time: 487 us; the launch traced here: 484 us
  blocking collectives  164 us (34%)
  waiting for transfers between devices  144 us (30%)
  matrix products  58.3 us (12%)
  local copies, waits for them, and re-layouts  52.2 us (11%)
  other arithmetic  27.4 us (6%)
  starting transfers between devices  22.9 us (5%)
  between operations  15.5 us (3%)
    all_to_all x5, waiting for transfers between devices, summed_on_arrival(): lax.all_to_all(pieces, axis, split_axis=0, concat_axis=0, tiled=True)  53.7 us
    reduce_scatter x1, waiting for transfers between devices, per_device(): lax.psum_scatter(jnp.dot(attended, out_weight, preferred_element_type=jnp...  37.8 us
    all_gather x1, blocking collectives, per_device(): lax.all_gather(w_qkv, 'dp', axis=1, tiled=True)  35.2 us
    all_gather x1, blocking collectives, per_device(): lax.all_gather(w_in, 'dp', axis=1, tiled=True)  34.9 us
    all_gather x1, blocking collectives, per_device(): lax.all_gather(w_down, 'dp', axis=1, tiled=True)  33.8 us
    all_gather x1, blocking collectives, per_device(): lax.all_gather(w_out, 'dp', axis=1, tiled=True)  31 us
    reduce_scatter x1, waiting for transfers between devices, per_device(): lax.psum_scatter(jnp.dot(hidden, down_weight, preferred_element_type=jnp....  28 us
    reduce_scatter x1, waiting for transfers between devices, per_device(): lax.psum_scatter(jnp.einsum('ctf,cdf->td', grad_gate_up, in_weight, prefe...  23.5 us
  transfers between devices with their start and end apart: 13, of which 7 were waited for; matrix products, arithmetic and copies ran while one was open for 19% of the time, Pallas kernels for 0%

commit v1 on v0

--- a/solution.py
+++ b/solution.py
@@ -1,6 +1,10 @@
+import functools
+
 import jax
 import jax.numpy as jnp
 from jax import lax
+from jax.experimental import pallas as pl
+from jax.experimental.pallas import tpu as pltpu
 from jax.sharding import PartitionSpec as P
 
 HEAD = 64
@@ -64,7 +68,7 @@
     )
 
 
-def per_device(tokens, gain_attn, gain_mlp, w_qkv, w_out, w_in, w_down, cotangent):
+def plain_layer(tokens, gain_attn, gain_mlp, w_qkv, w_out, w_in, w_down, cotangent):
     row_count = tokens.shape[0]
     group_rows = row_count * lax.axis_size("tensor")
     seq_count = group_rows // LEN
@@ -245,6 +249,436 @@
     )
 
 
+bf16 = jnp.bfloat16
+f32 = jnp.float32
+
+
+def mm(a, b):
+    return lax.dot_general(a, b, (((1,), (0,)), ((), ())), preferred_element_type=f32)
+
+
+def mm_nt(a, b):
+    return lax.dot_general(a, b, (((1,), (1,)), ((), ())), preferred_element_type=f32)
+
+
+def mm_tn(a, b):
+    return lax.dot_general(a, b, (((0,), (0,)), ((), ())), preferred_element_type=f32)
+
+
+def layer_kernel(
+    dp, rows, width, ff, ffp,
+    tokens, gain_a, gain_m, w_qkv, w_out, w_in, w_down, cotangent, cos_t, sin_t,
+    mixed, input_grad, gga_out, ggm_out, gqkv_out, gout_out, gin_out, gdown_out,
+    gpk, gbuf, pa, pb, nbuf, cbuf, mbuf, bbuf,
+    wgu, wdt, wot,
+    qs, qt, km, vm, probs, att, gatt, gproj, gqs, gkt, gvt,
+    hid, ggu,
+    xh1, xh2, res, gmix, keep,
+    s1, r1, s2, r2,
+    ga_s, ga_r, go_s, go_r, gb_s, gb_r, gt, gd_s, gd_r,
+    ss, rs,
+):
+    me = lax.axis_index("dp")
+    t = lax.axis_index("tensor")
+    x = lax.div(t, 2)
+    c = lax.rem(t, 2)
+    partner = x * 2 + (1 - c)
+    cross = (1 - x) * 2 + c
+    diag = (1 - x) * 2 + (1 - c)
+    shard = w_qkv.shape[1]
+    model = tokens.shape[1]
+    group = 4 * rows
+    counter = [0]
+    sent = []
+
+    def slot():
+        counter[0] += 1
+        return counter[0] - 1
+
+    def remote(source, target, k, d, tn):
+        return pltpu.make_async_remote_copy(
+            src_ref=source, dst_ref=target, send_sem=ss.at[k], recv_sem=rs.at[k],
+            device_id=(d, tn), device_id_type=pl.DeviceIdType.MESH,
+        )
+
+    def send(source, target, k, d, tn):
+        copy = remote(source, target, k, d, tn)
+        copy.start()
+        sent.append(copy)
+
+    barrier = pltpu.get_barrier_semaphore()
+    for i in range(1, dp):
+        pl.semaphore_signal(barrier, inc=1, device_id=(lax.rem(me + i, dp), t),
+                            device_id_type=pl.DeviceIdType.MESH)
+    for other in (partner, cross, diag):
+        pl.semaphore_signal(barrier, inc=1, device_id=(me, other),
+                            device_id_type=pl.DeviceIdType.MESH)
+
+    gpk[...] = jnp.zeros_like(gpk)
+    gpk[0:1, 0:shard] = gain_a[...].astype(f32)
+    gpk[1:2, 0:shard] = gain_m[...].astype(f32)
+    gbuf[me] = gpk[...]
+    own = [w_qkv[i] for i in range(3)] + [w_out[...].astype(f32).T.astype(bf16)]
+    pa[me] = jnp.concatenate(own, axis=1)
+    blank = jnp.zeros((shard, ffp - ff), bf16)
+    pb[me] = jnp.concatenate(
+        [w_in[0], blank, w_in[1], blank, w_down[...].astype(f32).T.astype(bf16), blank], axis=1)
+    cbuf[t] = cotangent[...]
+
+    pl.semaphore_wait(barrier, dp - 1 + 3)
+
+    def gather_dp(buf):
+        slots = []
+        for i in range(1, dp):
+            k = slot()
+            slots.append(k)
+            send(buf.at[me], buf.at[me], k, lax.rem(me + i, dp), t)
+        return slots
+
+    def gather_dp_wait(buf, slots):
+        for i in range(1, dp):
+            origin = lax.rem(me + dp - i, dp)
+            remote(buf.at[origin], buf.at[origin], slots[i - 1], origin, t).wait_recv()
+
+    def rows_start(buf):
+        slots = [slot(), slot(), slot()]
+        send(buf.at[t], buf.at[t], slots[1], me, cross)
+        send(buf.at[t], buf.at[t], slots[0], me, partner)
+        return slots
+
+    def rows_partner(buf, slots):
+        remote(buf.at[partner], buf.at[partner], slots[0], me, partner).wait_recv()
+
+    def rows_cross(buf, slots):
+        remote(buf.at[cross], buf.at[cross], slots[1], me, cross).wait_recv()
+        send(buf.at[cross], buf.at[cross], slots[2], me, partner)
+
+    def rows_diag(buf, slots):
+        remote(buf.at[diag], buf.at[diag], slots[2], me, partner).wait_recv()
+
+    def sum_init(n):
+        return (n, [slot(), slot(), slot()])
+
+    def sum_diag(state, value):
+        n, k = state
+        s1[n, 0] = value.astype(bf16)
+        send(s1.at[n, 0], r1.at[n, 0], k[0], me, partner)
+
+    def sum_partner(state, value):
+        n, k = state
+        s1[n, 1] = value.astype(bf16)
+        send(s1.at[n, 1], r1.at[n, 1], k[1], me, partner)
+
+    def sum_cross(state, value):
+        n, k = state
+        remote(s1.at[n, 0], r1.at[n, 0], k[0], me, partner).wait_recv()
+        s2[n] = (value + r1[n, 0].astype(f32)).astype(bf16)
+        send(s2.at[n], r2.at[n], k[2], me, cross)
+
+    def sum_own(state):
+        n, k = state
+        remote(s1.at[n, 1], r1.at[n, 1], k[1], me, partner).wait_recv()
+        remote(s2.at[n], r2.at[n], k[2], me, cross).wait_recv()
+        return r1[n, 1].astype(f32) + r2[n].astype(f32)
+
+    def norm_parts(value):
+        centred = value - jnp.mean(value, axis=-1, keepdims=True)
+        spread = jnp.mean(centred * centred, axis=-1, keepdims=True)
+        inverse = lax.rsqrt(spread + epsilon)
+        return centred * inverse, inverse
+
+    def norm_back(grad, gain, unit, inverse):
+        scaled = grad * gain
+        first = jnp.mean(scaled, axis=-1, keepdims=True)
+        second = jnp.mean(scaled * unit, axis=-1, keepdims=True)
+        return (inverse * (scaled - first - unit * second),
+                jnp.sum(grad * unit, axis=0, keepdims=True))
+
+    lanes = lax.broadcasted_iota(jnp.int32, (rows, 2 * width), 1)
+    low_half = lax.rem(lanes, HEAD) < HEAD // 2
+
+    def turn(value, b, sign):
+        other = jnp.where(low_half, pltpu.roll(value, 2 * width - HEAD // 2, 1),
+                          pltpu.roll(value, HEAD // 2, 1))
+        times = 2 * width // 128
+        cosine = jnp.concatenate([cos_t[b]] * times, axis=1)
+        sine = jnp.concatenate([sin_t[b]] * times, axis=1)
+        return value * cosine + sign * (other * sine)
+
+    heads = width // HEAD
+    scale = HEAD ** -0.5
+
+    gain_slots = gather_dp(gbuf)
+    pa_slots = gather_dp(pa)
+    unit, inverse1 = norm_parts(tokens[...].astype(f32))
+    xh1[...] = unit
+    gather_dp_wait(gbuf, gain_slots)
+    gain1 = jnp.concatenate([gbuf[j, 0:1, 0:shard] for j in range(dp)], axis=1)
+    gain2 = jnp.concatenate([gbuf[j, 1:2, 0:shard] for j in range(dp)], axis=1)
+    nbuf[t] = (unit * gain1).astype(bf16)
+    n_slots = rows_start(nbuf)
+    c_slots = rows_start(cbuf)
+    gather_dp_wait(pa, pa_slots)
+    pb_slots = gather_dp(pb)
+    wot[...] = pa[...].reshape(model, 4 * width)[:, 3 * width:]
+    head_of = lax.div(lax.broadcasted_iota(jnp.int32, (rows, width), 1), HEAD)
+
+    def project(b):
+        proj = mm(nbuf[b], pa[...].reshape(model, 4 * width)[:, : 3 * width])
+        turned = turn(proj[:, : 2 * width], b, 1.0)
+        q = turned[:, :width]
+        kk = turned[:, width:]
+        vv = proj[:, 2 * width:]
+        qs[b] = q.astype(bf16)
+        qt[b] = q.T.astype(bf16)
+        place = pl.ds(pl.multiple_of(b * rows, rows), rows)
+        for h in range(heads):
+            km[h, place, :] = jnp.where(head_of == h, kk, 0.0).astype(bf16)
+            vm[h, place, :] = jnp.where(head_of == h, vv, 0.0).astype(bf16)
+
+    project(t)
+    rows_partner(nbuf, n_slots)
+    project(partner)
+    rows_cross(nbuf, n_slots)
+    project(cross)
+    rows_diag(nbuf, n_slots)
+    project(diag)
+
+    def attend(i, carry):
+        q = qs[i]
+        acc = jnp.zeros((rows, width), f32)
+        for h in range(heads):
+            s = mm_nt(q, km[h]) * scale
+            e = jnp.exp(s - jnp.max(s, axis=-1, keepdims=True))
+            p = e * (1.0 / jnp.sum(e, axis=-1, keepdims=True))
+            probs[h, i] = p
+            acc = acc + mm(p.astype(bf16), vm[h])
+        att[i] = acc.astype(bf16)
+        return carry
+
+    lax.fori_loop(0, 4, attend, 0)
+
+    st = sum_init(0)
+    sum_diag(st, mm_nt(att[diag], wot[...]))
+    sum_partner(st, mm_nt(att[partner], wot[...]))
+    sum_cross(st, mm_nt(att[cross], wot[...]))
+    keep[0] = mm_nt(att[t], wot[...])
+    rows_cross(cbuf, c_slots)
+    rows_partner(cbuf, c_slots)
+    rows_diag(cbuf, c_slots)
+    gather_dp_wait(pb, pb_slots)
+    everything = pb[...].reshape(model, 3 * ffp)
+    wgu[...] = everything[:, : 2 * ffp]
+    wdt[...] = everything[:, 2 * ffp:]
+    res[...] = tokens[...].astype(f32) + (keep[0] + sum_own(st))
+    unit2, inverse2 = norm_parts(res[...])
+    xh2[...] = unit2
+    mbuf[t] = (unit2 * gain2).astype(bf16)
+    m_slots = rows_start(mbuf)
+
+    def mlp(b):
+        gu = mm(mbuf[b], wgu[...])
+        gate = gu[:, :ffp]
+        up = gu[:, ffp:]
+        phi = 0.5 * (1.0 + lax.erf(gate * 0.7071067811865476))
+        act = gate * phi
+        hid[b] = (act * up).astype(bf16)
+        gh = mm(cbuf[b], wdt[...])
+        slope = phi + gate * (jnp.exp(-0.5 * gate * gate) * 0.3989422804014327)
+        ggu[b, :, :ffp] = (gh * up * slope).astype(bf16)
+        ggu[b, :, ffp:] = (gh * act).astype(bf16)
+
+    st_g = sum_init(1)
+    mlp(t)
+    keep[0] = mm_nt(ggu[t], wgu[...])
+    rows_partner(mbuf, m_slots)
+    mlp(partner)
+    sum_partner(st_g, mm_nt(ggu[partner], wgu[...]))
+    rows_cross(mbuf, m_slots)
+    rows_diag(mbuf, m_slots)
+    mlp(diag)
+    sum_diag(st_g, mm_nt(ggu[diag], wgu[...]))
+    mlp(cross)
+    sum_cross(st_g, mm_nt(ggu[cross], wgu[...]))
+
+    mflat = mbuf[...].reshape(group, model)
+
+    def reduce_dp(buf, received):
+        slots = []
+        for i in range(1, dp):
+            k = slot()
+            slots.append(k)
+            peer = lax.rem(me + i, dp)
+            send(buf.at[peer], received.at[me], k, peer, t)
+        return slots
+
+    def reduce_dp_wait(buf, received, slots):
+        total = buf[me].astype(f32)
+        for i in range(1, dp):
+            origin = lax.rem(me + dp - i, dp)
+            remote(buf.at[origin], received.at[origin], slots[i - 1], origin, t).wait_recv()
+            total = total + received[origin].astype(f32)
+        return total
+
+    for part in range(2):
+        cut = slice(part * ffp, (part + 1) * ffp)
+        piece = mm_tn(mflat, ggu[:, :, cut].reshape(group, ffp))
+        gb_s[:, :, cut] = piece.astype(bf16).reshape(dp, shard, ffp)
+
+    gnm = keep[0] + sum_own(st_g)
+    back2, ggm = norm_back(gnm, gain2, xh2[...], inverse2)
+    gmix[...] = cotangent[...].astype(f32) + back2
+    bbuf[t] = gmix[...].astype(bf16)
+    b_slots = rows_start(bbuf)
+
+    st_d = sum_init(2)
+    sum_diag(st_d, mm_nt(hid[diag], wdt[...]))
+    sum_partner(st_d, mm_nt(hid[partner], wdt[...]))
+    piece = mm_tn(cbuf[...].reshape(group, model), hid[...].reshape(group, ffp))
+    gb_s[:, :, 2 * ffp:] = piece.astype(bf16).reshape(dp, shard, ffp)
+    gb_slots = reduce_dp(gb_s, gb_r)
+    rows_cross(bbuf, b_slots)
+    sum_cross(st_d, mm_nt(hid[cross], wdt[...]))
+    keep[0] = mm_nt(hid[t], wdt[...])
+    rows_partner(bbuf, b_slots)
+    rows_diag(bbuf, b_slots)
+
+    gkt[...] = jnp.zeros_like(gkt)
+    gvt[...] = jnp.zeros_like(gvt)
+
+    def attend_back(i, carry):
+        ga = mm(bbuf[i], wot[...])
+        gab = ga.astype(bf16)
+        gatt[i] = gab
+        gat = ga.T.astype(bf16)
+        acc = jnp.zeros((rows, width), f32)
+        for h in range(heads):
+            some = slice(h * HEAD, (h + 1) * HEAD)
+            gp = mm_nt(gab, vm[h])
+            p = probs[h, i]
+            inner = jnp.sum(p * gp, axis=-1, keepdims=True)
+            gs = (p * (gp - inner)).astype(bf16)
+            acc = acc + mm(gs, km[h])
+            gkt[some, :] += mm(qt[i, some, :], gs)
+            gvt[some, :] += mm(gat[some, :], p.astype(bf16))
+        gqs[i] = acc * scale
+        return carry
+
+    lax.fori_loop(0, 4, attend_back, 0)
+
+    piece = mm_tn(bbuf[...].reshape(group, model), att[...].reshape(group, width))
+    go_s[...] = piece.astype(bf16).reshape(dp, shard, width)
+    go_slots = reduce_dp(go_s, go_r)
+
+    def join(b, carry):
+        place = pl.ds(pl.multiple_of(b * rows, rows), rows)
+        gk = gkt[:, place].T * scale
+        back = turn(jnp.concatenate([gqs[b], gk], axis=1), b, -1.0)
+        gproj[b, :, : 2 * width] = back.astype(bf16)
+        gproj[b, :, 2 * width:] = gvt[:, place].T.astype(bf16)
+        return carry
+
+    lax.fori_loop(0, 4, join, 0)
+    wqkv = pa[...].reshape(model, 4 * width)[:, : 3 * width]
+    mixed[...] = (res[...] + (keep[0] + sum_own(st_d))).astype(bf16)
+    st_a = sum_init(3)
+    sum_diag(st_a, mm_nt(gproj[diag], wqkv))
+    sum_partner(st_a, mm_nt(gproj[partner], wqkv))
+    sum_cross(st_a, mm_nt(gproj[cross], wqkv))
+    piece = mm_tn(nbuf[...].reshape(group, model), gproj[...].reshape(group, 3 * width))
+    ga_s[...] = piece.astype(bf16).reshape(dp, shard, 3 * width)
+    ga_slots = reduce_dp(ga_s, ga_r)
+    keep[0] = mm_nt(gproj[t], wqkv)
+
+    total = reduce_dp_wait(gb_s, gb_r, gb_slots)
+    gin_out[0] = total[:, :ff]
+    gin_out[1] = total[:, ffp: ffp + ff]
+    gdown_out[...] = total[:, 2 * ffp:].T[:ff]
+    total = reduce_dp_wait(go_s, go_r, go_slots)
+    gout_out[...] = total.T
+
+    gna = keep[0] + sum_own(st_a)
+    back1, gga = norm_back(gna, gain1, xh1[...], inverse1)
+    gt[t] = jnp.concatenate([gga, ggm, jnp.zeros((6, model), f32)], axis=0)
+    tslots = [slot(), slot(), slot()]
+    for k, other in zip(tslots, (partner, cross, diag)):
+        send(gt.at[t], gt.at[t], k, me, other)
+    input_grad[...] = gmix[...] + back1
+    for k, other in zip(tslots, (partner, cross, diag)):
+        remote(gt.at[other], gt.at[other], k, me, other).wait_recv()
+    gains = (gt[0] + gt[1]) + (gt[2] + gt[3])
+    for j in range(dp):
+        gd_s[j, :, 0:shard] = gains[:, j * shard:(j + 1) * shard]
+        gd_s[j, :, shard:] = jnp.zeros((8, 128 - shard), f32)
+    gd_slots = reduce_dp(gd_s, gd_r)
+    total = reduce_dp_wait(ga_s, ga_r, ga_slots)
+    for i in range(3):
+        gqkv_out[i] = total[:, i * width:(i + 1) * width]
+    total = reduce_dp_wait(gd_s, gd_r, gd_slots)
+    gga_out[...] = total[0:1, :shard]
+    ggm_out[...] = total[1:2, :shard]
+    for copy in sent:
+        copy.wait_send()
+
+
+def per_device(tokens, gain_attn, gain_mlp, w_qkv, w_out, w_in, w_down, cotangent):
+    dp = lax.axis_size("dp")
+    rows, model = tokens.shape
+    shard, width = w_qkv.shape[1:]
+    ff = w_in.shape[2]
+    one_sequence = lax.axis_size("tensor") == 4 and rows * 4 == LEN
+    if not (one_sequence and shard % 16 == 0 and shard <= 128 and 2 * width % 128 == 0):
+        return plain_layer(tokens, gain_attn, gain_mlp, w_qkv, w_out, w_in, w_down, cotangent)
+    ffp = -(-ff // 128) * 128
+    cosine, sine = rotary(LEN)
+    cosine, sine = cosine[:, 0], sine[:, 0]
+    cos_t = jnp.concatenate([cosine] * 4, axis=1).reshape(4, rows, 2 * HEAD)
+    sin_t = jnp.concatenate([-sine, sine] * 2, axis=1).reshape(4, rows, 2 * HEAD)
+    vmem = pltpu.VMEM
+    scratch = [
+        vmem((8, 128), f32), vmem((dp, 8, 128), f32),
+        vmem((dp, shard, 4 * width), bf16), vmem((dp, shard, 3 * ffp), bf16),
+        vmem((4, rows, model), bf16), vmem((4, rows, model), bf16),
+        vmem((4, rows, model), bf16), vmem((4, rows, model), bf16),
+        vmem((model, 2 * ffp), bf16), vmem((model, ffp), bf16), vmem((model, width), bf16),
+        vmem((4, rows, width), bf16), vmem((4, width, rows), bf16),
+        vmem((width // HEAD, LEN, width), bf16), vmem((width // HEAD, LEN, width), bf16),
+        vmem((width // HEAD, 4, rows, LEN), f32),
+        vmem((4, rows, width), bf16), vmem((4, rows, width), bf16),
+        vmem((4, rows, 3 * width), bf16), vmem((4, rows, width), f32),
+        vmem((width, LEN), f32), vmem((width, LEN), f32),
+        vmem((4, rows, ffp), bf16), vmem((4, rows, 2 * ffp), bf16),
+        vmem((rows, model), f32), vmem((rows, model), f32),
+        vmem((rows, model), f32), vmem((rows, model), f32), vmem((1, rows, model), f32),
+        vmem((4, 2, rows, model), bf16), vmem((4, 2, rows, model), bf16),
+        vmem((4, rows, model), bf16), vmem((4, rows, model), bf16),
+        vmem((dp, shard, 3 * width), bf16), vmem((dp, shard, 3 * width), bf16),
+        vmem((dp, shard, width), bf16), vmem((dp, shard, width), bf16),
+        vmem((dp, shard, 3 * ffp), bf16), vmem((dp, shard, 3 * ffp), bf16),
+        vmem((4, 8, model), f32), vmem((dp, 8, 128), f32), vmem((dp, 8, 128), f32),
+        pltpu.SemaphoreType.DMA((7 * (dp - 1) + 27,)),
+        pltpu.SemaphoreType.DMA((7 * (dp - 1) + 27,)),
+    ]
+    whole = pl.BlockSpec(memory_space=pltpu.VMEM)
+    shape = jax.ShapeDtypeStruct
+    outs = pl.pallas_call(
+        functools.partial(layer_kernel, dp, rows, width, ff, ffp),
+        out_shape=[
+            shape((rows, model), bf16), shape((rows, model), f32),
+            shape((1, shard), f32), shape((1, shard), f32),
+            shape(w_qkv.shape, f32), shape(w_out.shape, f32),
+            shape(w_in.shape, f32), shape(w_down.shape, f32),
+        ],
+        in_specs=[whole] * 10,
+        out_specs=[whole] * 8,
+        scratch_shapes=scratch,
+        compiler_params=pltpu.CompilerParams(
+            collective_id=0, has_side_effects=True, vmem_limit_bytes=62 * 1024 * 1024),
+    )(tokens, gain_attn[None], gain_mlp[None], w_qkv, w_out, w_in, w_down, cotangent, cos_t, sin_t)
+    mixed, input_grad, gga, ggm, gqkv, gout, gin, gdown = outs
+    return mixed, input_grad, gga[0], ggm[0], gqkv, gout, gin, gdown
+
+
 def solution(mesh):
     placed = (
         P(("dp", "tensor"), None),

time: 487 us -> 185 us (0.38)
  Pallas kernels: 0 us -> 174 us
  blocking collectives: 164 us -> 0 us
  waiting for transfers between devices: 144 us -> 0 us
  matrix products: 58.3 us -> 0 us
  local copies, waits for them, and re-layouts: 52.2 us -> 7.19 us
  other arithmetic: 27.4 us -> 3.77 us
  starting transfers between devices: 22.9 us -> 0 us
  between operations: 15.5 us -> 0.68 us
    pallas_call x0 -> x1, Pallas kernels: none -> 174 us  [per_device(): pl.pallas_call(functools.partial(layer_kernel, dp, rows, width, ff, ffp),...]
    all_gather x4 -> x0, blocking collectives: 135 us -> none  [the longest x1 35.2 us: per_device(): lax.all_gather(w_qkv, 'dp', axis=1, tiled=True)]
    reduce_scatter x4 -> x0, waiting for transfers between devices: 89.3 us -> none  [the longest x1 37.8 us: per_device(): lax.psum_scatter(jnp.dot(attended, out_weight, preferred_element_type=jnp...]
    dot_general x25 -> x0, matrix products: 55.8 us -> none  [the longest x2 5.77 us: attend_back(): jnp.einsum('sqhd,skhd->shqk', grad_block, values, preferred_element_type=...]
    all_to_all x5 -> x0, waiting for transfers between devices: 53.7 us -> none  [summed_on_arrival(): lax.all_to_all(pieces, axis, split_axis=0, concat_axis=0, tiled=True)]
    unnamed x1 -> x0, blocking collectives: 23.1 us -> none
    all_to_all x5 -> x0, starting transfers between devices: 22.3 us -> none  [summed_on_arrival(): lax.all_to_all(pieces, axis, split_axis=0, concat_axis=0, tiled=True)]
    dynamic_update_slice x4 -> x0, local copies, waits for them, and re-layouts: 17 us -> none  [per_device(): lax.scan(attend_back, (zero_state, zero_state), (query_blocks, split_bloc...]
  transfers between devices with their start and end apart: 13 -> 0, of which waited for: 7 -> 0; matrix products, arithmetic and copies ran while one was open for 19% -> 0% of each run, Pallas kernels for 0% -> 0%
where the time goes in v1:
time: 185 us
  Pallas kernels  174 us (94%)
  local copies, waits for them, and re-layouts  7.19 us (4%)
  other arithmetic  3.77 us (2%)
    pallas_call x1, Pallas kernels, per_device(): pl.pallas_call(functools.partial(layer_kernel, dp, rows, width, ff, ffp),...  174 us
    unnamed x22, local copies, waits for them, and re-layouts  7.19 us

profile of v1, /device:TPU:0, one launch (start us, length us, event | category | flops | bytes accessed | tf_op | source)
XLA Modules:
  0.0 185.3 jit_solution(4159774473797954012)
XLA Ops:
  0.7 1.9 %fusion = (f32[4,256,32]{2,1,0:T(8,128)S(1)}, f32[4,256,32]{2,1,0:T(8,128)S(1)}, f32[4,256,32]{2,1,0:T(8,128)S(1)}) fusion(f32[32]{0:T(128)S(1)} %multiply_power_fusion, f32[4,256]{1,0:T(4,128)S(1)} %multiply_add_fusion), kind=kLoop, calls=%fused_computation.4 | loop fusion | flops 65536 | bytes 397440 | tf_op jit(solution)/shard_map/neg | solution.py:636
  2.6 1.9 %pad_maximum_fusion = (f32[4,256,128]{2,1,0:T(8,128)}, f32[4,256,128]{2,1,0:T(8,128)}) fusion(f32[4,256,32]{2,1,0:T(8,128)S(1)} %get-tuple-element.26, f32[4,256,32]{2,1,0:T(8,128)S(1)} %get-tuple-element.25, f32[4,256,32]{2,1,0:T(8,128)S(1)} %get-tuple-element.24), kind=kLoop, calls=%fused_computation.2 | loop fusion | flops 786432 | bytes 1441792 | tf_op jit(solution)/shard_map/concatenate | solution.py:635
  4.4 173.6 %shard_map.143 = (bf16[256,768]{1,0:T(8,128)(2,1)}, f32[256,768]{1,0:T(8,128)}, f32[1,96]{1,0:T(1,128)}, f32[1,96]{1,0:T(1,128)}, f32[3,96,192]{2,1,0:T(8,128)},...) custom-call(bf16[256,768]{1,0:T(8,128)(2,1)} %tokens.1, bf16[1,96]{1,0:T(2,128)(2,1)} %bitcast.4, ...), custom_call_target="tpu_custom_call" | custom-call | tf_op jit(solution)/shard_map/pallas_call | solution.py:664
  178.1 0.0 copy-start
  178.1 1.8 copy.24
  179.9 0.0 copy-done
  179.9 0.0 copy-start.6
  179.9 0.0 copy-start.2
  179.9 0.9 copy.25
  180.8 0.0 copy-done.6
  180.8 0.0 copy-start.5
  180.8 0.5 copy.26
  181.3 0.2 copy-done.5
  181.5 0.5 copy.27
  182.0 0.0 copy-done.2
  182.0 0.0 copy-start.4
  182.0 0.0 copy-start.1
  182.0 0.7 copy.28
  182.7 0.2 copy-done.4
  182.9 0.6 copy.29
  183.6 0.0 copy-done.1
  183.6 0.0 copy-start.3
  183.6 0.7 copy.30
  184.3 0.3 copy-done.3
  184.6 0.7 copy.31
  (2 shorter events, 0.0 us)
Async XLA Ops:
  178.1 1.9 copy-start
  179.9 0.9 copy-start.6
  179.9 2.1 %copy-start.2 = (f32[3,96,192]{2,1,0:T(8,128)S(1)}, f32[3,96,192]{2,1,0:T(8,128)}, u32[]{:S(2)}) copy-start(f32[3,96,192]{2,1,0:T(8,128)} %get-tuple-element.41) | copy-start | bytes 663556
  180.8 0.7 copy-start.5
  182.0 1.0 copy-start.4
  182.0 1.6 copy-start.1
  183.6 1.0 copy-start.3

commit v2 on v1

--- a/solution.py
+++ b/solution.py
@@ -1,5 +1,6 @@
 import functools
 
+import numpy as np
 import jax
 import jax.numpy as jnp
 from jax import lax
@@ -275,7 +276,7 @@
     hid, ggu,
     xh1, xh2, res, gmix, keep,
     s1, r1, s2, r2,
-    ga_s, ga_r, go_s, go_r, gb_s, gb_r, gt, gd_s, gd_r,
+    ga_s, ga_y, ga_z, go_s, go_y, go_z, gb_s, gb_y, gb_z, gf_s, gf_y, gf_z, gt, gd_s, gd_r,
     ss, rs,
 ):
     me = lax.axis_index("dp")
@@ -327,7 +328,56 @@
 
     pl.semaphore_wait(barrier, dp - 1 + 3)
 
+    zc = lax.div(me, 2)
+    yc = lax.rem(me, 2)
+    deep = dp // 2
+    beside = zc * 2 + (1 - yc)
+
+    def column(i, y):
+        return lax.rem(zc + i, deep) * 2 + y
+
     def gather_dp(buf):
+        slots = [slot() for _ in range(dp - 1)]
+        send(buf.at[me], buf.at[me], slots[0], beside, t)
+        for i in range(1, deep):
+            send(buf.at[me], buf.at[me], slots[i], column(i, yc), t)
+        return slots
+
+    def gather_dp_pass(buf, slots):
+        for i in range(1, deep):
+            origin = column(deep - i, yc)
+            remote(buf.at[origin], buf.at[origin], slots[i], origin, t).wait_recv()
+            send(buf.at[origin], buf.at[origin], slots[deep - 1 + i], beside, t)
+
+    def gather_dp_end(buf, slots):
+        remote(buf.at[beside], buf.at[beside], slots[0], beside, t).wait_recv()
+        for i in range(1, deep):
+            origin = column(deep - i, 1 - yc)
+            remote(buf.at[origin], buf.at[origin], slots[deep - 1 + i], beside, t).wait_recv()
+
+    def reduce_start(buf, over_y):
+        slots = [slot() for _ in range(dp - 1)]
+        for i in (*range(1, deep), 0):
+            send(buf.at[column(i, 1 - yc)], over_y.at[i], slots[i], beside, t)
+        return slots
+
+    def reduce_pass(buf, over_y, over_z, slots):
+        for i in range(1, deep):
+            to = column(i, yc)
+            remote(buf.at[to], over_y.at[i], slots[i], beside, t).wait_recv()
+            buf[to] = (buf[to].astype(f32) + over_y[i].astype(f32)).astype(bf16)
+            send(buf.at[to], over_z.at[i], slots[deep - 1 + i], to, t)
+
+    def reduce_end(buf, over_y, over_z, slots):
+        remote(buf.at[me], over_y.at[0], slots[0], beside, t).wait_recv()
+        total = buf[me].astype(f32) + over_y[0].astype(f32)
+        for i in range(1, deep):
+            origin = column(deep - i, yc)
+            remote(buf.at[origin], over_z.at[i], slots[deep - 1 + i], origin, t).wait_recv()
+            total = total + over_z[i].astype(f32)
+        return total
+
+    def gather_small(buf):
         slots = []
         for i in range(1, dp):
             k = slot()
@@ -335,7 +385,7 @@
             send(buf.at[me], buf.at[me], k, lax.rem(me + i, dp), t)
         return slots
 
-    def gather_dp_wait(buf, slots):
+    def gather_small_wait(buf, slots):
         for i in range(1, dp):
             origin = lax.rem(me + dp - i, dp)
             remote(buf.at[origin], buf.at[origin], slots[i - 1], origin, t).wait_recv()
@@ -408,17 +458,18 @@
     heads = width // HEAD
     scale = HEAD ** -0.5
 
-    gain_slots = gather_dp(gbuf)
+    gain_slots = gather_small(gbuf)
     pa_slots = gather_dp(pa)
     unit, inverse1 = norm_parts(tokens[...].astype(f32))
     xh1[...] = unit
-    gather_dp_wait(gbuf, gain_slots)
+    gather_small_wait(gbuf, gain_slots)
     gain1 = jnp.concatenate([gbuf[j, 0:1, 0:shard] for j in range(dp)], axis=1)
     gain2 = jnp.concatenate([gbuf[j, 1:2, 0:shard] for j in range(dp)], axis=1)
     nbuf[t] = (unit * gain1).astype(bf16)
     n_slots = rows_start(nbuf)
     c_slots = rows_start(cbuf)
-    gather_dp_wait(pa, pa_slots)
+    gather_dp_pass(pa, pa_slots)
+    gather_dp_end(pa, pa_slots)
     pb_slots = gather_dp(pb)
     wot[...] = pa[...].reshape(model, 4 * width)[:, 3 * width:]
     head_of = lax.div(lax.broadcasted_iota(jnp.int32, (rows, width), 1), HEAD)
@@ -444,7 +495,7 @@
     rows_diag(nbuf, n_slots)
     project(diag)
 
-    def attend(i, carry):
+    def attend(i):
         q = qs[i]
         acc = jnp.zeros((rows, width), f32)
         for h in range(heads):
@@ -454,27 +505,34 @@
             probs[h, i] = p
             acc = acc + mm(p.astype(bf16), vm[h])
         att[i] = acc.astype(bf16)
-        return carry
-
-    lax.fori_loop(0, 4, attend, 0)
+
+    def attend_two(first, second):
+        def step(i, carry):
+            attend(first + i * (second - first))
+            return carry
+
+        lax.fori_loop(0, 2, step, 0)
 
     st = sum_init(0)
+    attend_two(diag, cross)
     sum_diag(st, mm_nt(att[diag], wot[...]))
+    sum_cross(st, mm_nt(att[cross], wot[...]))
+    attend_two(partner, t)
     sum_partner(st, mm_nt(att[partner], wot[...]))
-    sum_cross(st, mm_nt(att[cross], wot[...]))
     keep[0] = mm_nt(att[t], wot[...])
+    gather_dp_pass(pb, pb_slots)
     rows_cross(cbuf, c_slots)
     rows_partner(cbuf, c_slots)
     rows_diag(cbuf, c_slots)
-    gather_dp_wait(pb, pb_slots)
-    everything = pb[...].reshape(model, 3 * ffp)
-    wgu[...] = everything[:, : 2 * ffp]
-    wdt[...] = everything[:, 2 * ffp:]
     res[...] = tokens[...].astype(f32) + (keep[0] + sum_own(st))
     unit2, inverse2 = norm_parts(res[...])
     xh2[...] = unit2
     mbuf[t] = (unit2 * gain2).astype(bf16)
     m_slots = rows_start(mbuf)
+    gather_dp_end(pb, pb_slots)
+    everything = pb[...].reshape(model, 3 * ffp)
+    wgu[...] = everything[:, : 2 * ffp]
+    wdt[...] = everything[:, 2 * ffp:]
 
     def mlp(b):
         gu = mm(mbuf[b], wgu[...])
@@ -503,7 +561,7 @@
 
     mflat = mbuf[...].reshape(group, model)
 
-    def reduce_dp(buf, received):
+    def reduce_small(buf, received):
         slots = []
         for i in range(1, dp):
             k = slot()
@@ -512,7 +570,7 @@
             send(buf.at[peer], received.at[me], k, peer, t)
         return slots
 
-    def reduce_dp_wait(buf, received, slots):
+    def reduce_small_wait(buf, received, slots):
         total = buf[me].astype(f32)
         for i in range(1, dp):
             origin = lax.rem(me + dp - i, dp)
@@ -524,6 +582,7 @@
         cut = slice(part * ffp, (part + 1) * ffp)
         piece = mm_tn(mflat, ggu[:, :, cut].reshape(group, ffp))
         gb_s[:, :, cut] = piece.astype(bf16).reshape(dp, shard, ffp)
+    gb_slots = reduce_start(gb_s, gb_y)
 
     gnm = keep[0] + sum_own(st_g)
     back2, ggm = norm_back(gnm, gain2, xh2[...], inverse2)
@@ -535,14 +594,18 @@
     sum_diag(st_d, mm_nt(hid[diag], wdt[...]))
     sum_partner(st_d, mm_nt(hid[partner], wdt[...]))
     piece = mm_tn(cbuf[...].reshape(group, model), hid[...].reshape(group, ffp))
-    gb_s[:, :, 2 * ffp:] = piece.astype(bf16).reshape(dp, shard, ffp)
-    gb_slots = reduce_dp(gb_s, gb_r)
+    gf_s[...] = piece.astype(bf16).reshape(dp, shard, ffp)
+    gf_slots = reduce_start(gf_s, gf_y)
     rows_cross(bbuf, b_slots)
     sum_cross(st_d, mm_nt(hid[cross], wdt[...]))
     keep[0] = mm_nt(hid[t], wdt[...])
     rows_partner(bbuf, b_slots)
     rows_diag(bbuf, b_slots)
 
+    piece = mm_tn(bbuf[...].reshape(group, model), att[...].reshape(group, width))
+    go_s[...] = piece.astype(bf16).reshape(dp, shard, width)
+    go_slots = reduce_start(go_s, go_y)
+    reduce_pass(gb_s, gb_y, gb_z, gb_slots)
     gkt[...] = jnp.zeros_like(gkt)
     gvt[...] = jnp.zeros_like(gvt)
 
@@ -566,10 +629,6 @@
 
     lax.fori_loop(0, 4, attend_back, 0)
 
-    piece = mm_tn(bbuf[...].reshape(group, model), att[...].reshape(group, width))
-    go_s[...] = piece.astype(bf16).reshape(dp, shard, width)
-    go_slots = reduce_dp(go_s, go_r)
-
     def join(b, carry):
         place = pl.ds(pl.multiple_of(b * rows, rows), rows)
         gk = gkt[:, place].T * scale
@@ -579,6 +638,8 @@
         return carry
 
     lax.fori_loop(0, 4, join, 0)
+    reduce_pass(gf_s, gf_y, gf_z, gf_slots)
+    reduce_pass(go_s, go_y, go_z, go_slots)
     wqkv = pa[...].reshape(model, 4 * width)[:, : 3 * width]
     mixed[...] = (res[...] + (keep[0] + sum_own(st_d))).astype(bf16)
     st_a = sum_init(3)
@@ -587,14 +648,16 @@
     sum_cross(st_a, mm_nt(gproj[cross], wqkv))
     piece = mm_tn(nbuf[...].reshape(group, model), gproj[...].reshape(group, 3 * width))
     ga_s[...] = piece.astype(bf16).reshape(dp, shard, 3 * width)
-    ga_slots = reduce_dp(ga_s, ga_r)
+    ga_slots = reduce_start(ga_s, ga_y)
     keep[0] = mm_nt(gproj[t], wqkv)
 
-    total = reduce_dp_wait(gb_s, gb_r, gb_slots)
+    total = reduce_end(gb_s, gb_y, gb_z, gb_slots)
     gin_out[0] = total[:, :ff]
     gin_out[1] = total[:, ffp: ffp + ff]
-    gdown_out[...] = total[:, 2 * ffp:].T[:ff]
-    total = reduce_dp_wait(go_s, go_r, go_slots)
+    reduce_pass(ga_s, ga_y, ga_z, ga_slots)
+    total = reduce_end(gf_s, gf_y, gf_z, gf_slots)
+    gdown_out[...] = total.T[:ff]
+    total = reduce_end(go_s, go_y, go_z, go_slots)
     gout_out[...] = total.T
 
     gna = keep[0] + sum_own(st_a)
@@ -610,15 +673,20 @@
     for j in range(dp):
         gd_s[j, :, 0:shard] = gains[:, j * shard:(j + 1) * shard]
         gd_s[j, :, shard:] = jnp.zeros((8, 128 - shard), f32)
-    gd_slots = reduce_dp(gd_s, gd_r)
-    total = reduce_dp_wait(ga_s, ga_r, ga_slots)
+    gd_slots = reduce_small(gd_s, gd_r)
+    total = reduce_end(ga_s, ga_y, ga_z, ga_slots)
     for i in range(3):
         gqkv_out[i] = total[:, i * width:(i + 1) * width]
-    total = reduce_dp_wait(gd_s, gd_r, gd_slots)
+    total = reduce_small_wait(gd_s, gd_r, gd_slots)
     gga_out[...] = total[0:1, :shard]
     ggm_out[...] = total[1:2, :shard]
     for copy in sent:
         copy.wait_send()
+
+
+def move_kernel(*refs):
+    for i in range(8):
+        refs[8 + i][...] = refs[i][...]
 
 
 def per_device(tokens, gain_attn, gain_mlp, w_qkv, w_out, w_in, w_down, cotangent):
@@ -627,14 +695,20 @@
     shard, width = w_qkv.shape[1:]
     ff = w_in.shape[2]
     one_sequence = lax.axis_size("tensor") == 4 and rows * 4 == LEN
-    if not (one_sequence and shard % 16 == 0 and shard <= 128 and 2 * width % 128 == 0):
+    if not (one_sequence and dp == 8 and shard % 16 == 0 and shard <= 128 and 2 * width % 128 == 0):
         return plain_layer(tokens, gain_attn, gain_mlp, w_qkv, w_out, w_in, w_down, cotangent)
     ffp = -(-ff // 128) * 128
-    cosine, sine = rotary(LEN)
-    cosine, sine = cosine[:, 0], sine[:, 0]
-    cos_t = jnp.concatenate([cosine] * 4, axis=1).reshape(4, rows, 2 * HEAD)
-    sin_t = jnp.concatenate([-sine, sine] * 2, axis=1).reshape(4, rows, 2 * HEAD)
+    half = np.arange(HEAD // 2, dtype=np.float32)
+    frequency = np.float32(rope_base) ** (np.float32(-2.0) * half / np.float32(HEAD))
+    angles = np.arange(LEN, dtype=np.float32)[:, None] * frequency[None, :].astype(np.float32)
+    cosine, sine = np.cos(angles), np.sin(angles)
+    cos_t = np.concatenate([cosine] * 4, axis=1).reshape(4, rows, 2 * HEAD)
+    sin_t = np.concatenate([-sine, sine] * 2, axis=1).reshape(4, rows, 2 * HEAD)
     vmem = pltpu.VMEM
+
+    def reduction(columns):
+        return [vmem((count, shard, columns), bf16) for count in (dp, dp // 2, dp // 2)]
+
     scratch = [
         vmem((8, 128), f32), vmem((dp, 8, 128), f32),
         vmem((dp, shard, 4 * width), bf16), vmem((dp, shard, 3 * ffp), bf16),
@@ -652,12 +726,10 @@
         vmem((rows, model), f32), vmem((rows, model), f32), vmem((1, rows, model), f32),
         vmem((4, 2, rows, model), bf16), vmem((4, 2, rows, model), bf16),
         vmem((4, rows, model), bf16), vmem((4, rows, model), bf16),
-        vmem((dp, shard, 3 * width), bf16), vmem((dp, shard, 3 * width), bf16),
-        vmem((dp, shard, width), bf16), vmem((dp, shard, width), bf16),
-        vmem((dp, shard, 3 * ffp), bf16), vmem((dp, shard, 3 * ffp), bf16),
+        *reduction(3 * width), *reduction(width), *reduction(2 * ffp), *reduction(ffp),
         vmem((4, 8, model), f32), vmem((dp, 8, 128), f32), vmem((dp, 8, 128), f32),
-        pltpu.SemaphoreType.DMA((7 * (dp - 1) + 27,)),
-        pltpu.SemaphoreType.DMA((7 * (dp - 1) + 27,)),
+        pltpu.SemaphoreType.DMA((8 * (dp - 1) + 27,)),
+        pltpu.SemaphoreType.DMA((8 * (dp - 1) + 27,)),
     ]
     whole = pl.BlockSpec(memory_space=pltpu.VMEM)
     shape = jax.ShapeDtypeStruct
@@ -675,6 +747,12 @@
         compiler_params=pltpu.CompilerParams(
             collective_id=0, has_side_effects=True, vmem_limit_bytes=62 * 1024 * 1024),
     )(tokens, gain_attn[None], gain_mlp[None], w_qkv, w_out, w_in, w_down, cotangent, cos_t, sin_t)
+    outs = pl.pallas_call(
+        move_kernel,
+        out_shape=[shape(o.shape, o.dtype) for o in outs],
+        in_specs=[whole] * 8,
+        out_specs=[whole] * 8,
+    )(*outs)
     mixed, input_grad, gga, ggm, gqkv, gout, gin, gdown = outs
     return mixed, input_grad, gga[0], ggm[0], gqkv, gout, gin, gdown
 

time: 185 us -> 135 us (0.73)
  Pallas kernels: 174 us -> 134 us
  local copies, waits for them, and re-layouts: 7.19 us -> 0 us
  other arithmetic: 3.77 us -> 0 us
    pallas_call x1, Pallas kernels: 174 us -> 131 us  [per_device(): pl.pallas_call(functools.partial(layer_kernel, dp, rows, width, ff, ffp),...]
    unnamed x22 -> x0, local copies, waits for them, and re-layouts: 7.19 us -> none
    pallas_call x0 -> x1, Pallas kernels: none -> 2.82 us  [per_device(): pl.pallas_call(move_kernel, out_shape=[shape(o.shape, o.dtype) for o in o...]
    neg x1 -> x0, other arithmetic: 1.9 us -> none  [per_device(): -sine]
    concatenate x1 -> x0, other arithmetic: 1.85 us -> none  [per_device(): cos_t = jnp.concatenate([cosine] * 4, axis=1).reshape(4, rows, 2 * HEAD)]
where the time goes in v2:
time: 135 us
  Pallas kernels  134 us (99%)
    pallas_call x1, Pallas kernels, per_device(): pl.pallas_call(functools.partial(layer_kernel, dp, rows, width, ff, ffp),...  131 us
    pallas_call x1, Pallas kernels, per_device(): pl.pallas_call(move_kernel, out_shape=[shape(o.shape, o.dtype) for o in o...  2.82 us

profile of v2, /device:TPU:0, one launch (start us, length us, event | category | flops | bytes accessed | tf_op | source)
XLA Modules:
  0.0 134.9 jit_solution(17129266487787309087)
XLA Ops:
  0.6 131.4 %shard_map.161 = (bf16[256,768]{1,0:T(8,128)(2,1)}, f32[256,768]{1,0:T(8,128)}, f32[1,96]{1,0:T(1,128)}, f32[1,96]{1,0:T(1,128)}, f32[3,96,192]{2,1,0:T(8,128)},...) custom-call(bf16[256,768]{1,0:T(8,128)(2,1)} %tokens.1, bf16[1,96]{1,0:T(2,128)(2,1)} %bitcast.4, ...), custom_call_target="tpu_custom_call" | custom-call | tf_op jit(solution)/shard_map/pallas_call | solution.py:736
  132.0 2.8 %shard_map.162 = (bf16[256,768]{1,0:T(8,128)(2,1)}, f32[256,768]{1,0:T(8,128)}, f32[1,96]{1,0:T(1,128)}, f32[1,96]{1,0:T(1,128)}, f32[3,96,192]{2,1,0:T(8,128)},...) custom-call(bf16[256,768]{1,0:T(8,128)(2,1)} %get-tuple-element.24.refs_0_, ...), custom_call_target="tpu_custom_call" | custom-call | tf_op jit(solution)/shard_map/pallas_call | solution.py:750
